TPU v7x, 256 devices: a whole 4x4x8 slice. The times are simulated.
256 devices in a mesh: row: 16 (over y, x), col: 16 (over z, core).
Axes of the slice: x: 4, y: 4, z: 8, core: 2. Of those that a mesh axis runs over, the one named last changes fastest.
Arguments:
- source_points: float32 [24576, 128], P('row'), may hold values from -6 to 6
- target_points: float32 [24576, 128], P('col'), may hold values from -6 to 6
- source_pot: float32 [24576], P('row'), may hold values from -2 to 65
- target_pot: float32 [24576], P('col'), may hold values from -2 to 65
- source_cot: float32 [24576], P('row'), may hold values from -6 to 6
- target_cot: float32 [24576], P('col'), may hold values from -6 to 6
Outputs:
- grad_source: float32 [24576, 128], P(('row', 'col'))
- grad_target: float32 [24576, 128], P(('col', 'row'))
All inputs are finite; a program needn't handle non-finite values.
Results may differ from a plain program's by a relative error of at most 0.0003.
Values sent between devices are 32-bit elements; how exact they have to be, the bound alone decides.
A program may use at most 128 MiB of HBM per device.

v0:
```python
import jax
import jax.numpy as jnp
from jax import lax
from jax.sharding import PartitionSpec as P

ITERS = 3


epsilon = 0.5


def pair_distance(query, others):
    inner = lax.dot_general(
        query,
        others,
        (((1,), (1,)), ((), ())),
        precision=lax.Precision.HIGHEST,
        preferred_element_type=jnp.float32,
    )
    return (
        0.5 * jnp.sum(query * query, axis=1)[:, None]
        + 0.5 * jnp.sum(others * others, axis=1)[None, :]
        - inner
    )


def hot_dot(left, right):
    return jnp.dot(left, right, precision=lax.Precision.HIGHEST, preferred_element_type=jnp.float32)


def shards(source_points, target_points, source_pot, target_pot, source_cot, target_cot):
    distance = pair_distance(source_points, target_points)
    row_logits = (target_pot[None, :] - distance) / epsilon
    col_logits = (source_pot[:, None] - distance) / epsilon
    row_peak = lax.pmax(jnp.max(row_logits, axis=1), "col")
    col_peak = lax.pmax(jnp.max(col_logits, axis=0), "row")
    row_total = lax.psum(jnp.sum(jnp.exp(row_logits - row_peak[:, None]), axis=1), "col")
    col_total = lax.psum(jnp.sum(jnp.exp(col_logits - col_peak[None, :]), axis=0), "row")
    row_norm = row_peak + jnp.log(row_total)
    col_norm = col_peak + jnp.log(col_total)
    source_adj = source_cot
    target_adj = target_cot
    for iteration in range(ITERS):
        toward_fresh = pair_distance(source_points, target_points)
        target_push = hot_dot(
            source_adj, jnp.exp((target_pot[None, :] - toward_fresh) / epsilon - row_norm[:, None])
        )
        target_adj = target_cot - lax.psum(target_push, "row")
        fresh = pair_distance(source_points, target_points)
        source_push = hot_dot(
            jnp.exp((source_pot[:, None] - fresh) / epsilon - col_norm[None, :]), target_adj
        )
        source_adj = source_cot - lax.psum(source_push, "col")
    block = source_points
    block_adj = source_adj
    block_pot = source_pot
    block_norm = row_norm
    near = pair_distance(source_points, target_points)
    own_kernel = jnp.exp((target_pot[None, :] - near) / epsilon - block_norm[:, None])
    other_kernel = jnp.exp((block_pot[:, None] - near) / epsilon - col_norm[None, :])
    weight = block_adj[:, None] * own_kernel + target_adj[None, :] * other_kernel
    grad_source = lax.psum_scatter(
        block * jnp.sum(weight, axis=1)[:, None] - hot_dot(weight, target_points),
        "col",
        scatter_dimension=0,
        tiled=True,
    )
    block = target_points
    block_adj = target_adj
    block_pot = target_pot
    block_norm = col_norm
    near = pair_distance(target_points, source_points)
    own_kernel = jnp.exp((source_pot[None, :] - near) / epsilon - block_norm[:, None])
    other_kernel = jnp.exp((block_pot[:, None] - near) / epsilon - row_norm[None, :])
    weight = block_adj[:, None] * own_kernel + source_adj[None, :] * other_kernel
    grad_target = lax.psum_scatter(
        block * jnp.sum(weight, axis=1)[:, None] - hot_dot(weight, source_points),
        "row",
        scatter_dimension=0,
        tiled=True,
    )
    return (grad_source, grad_target)


def solution(mesh):
    in_specs = (P("row", None), P("col", None), P("row"), P("col"), P("row"), P("col"))
    out_specs = (P(("row", "col"), None), P(("col", "row"), None))
    return jax.shard_map(shards, mesh=mesh, in_specs=in_specs, out_specs=out_specs, check_vma=False)
```

profile of v0, /device:TPU:1, one launch (start us, length us, event | category | flops | bytes accessed | tf_op | source)
XLA Modules:
  0.0 571.1 jit_solution(15308066358049667646)
XLA Ops:
  9.3 1.4 multiply_reduce_fusion
  10.8 13.5 %fusion = (f32[1536]{0:T(1024)S(1)}, f32[1536]{0:T(1024)S(1)}, f32[1536,1536]{0,1:T(8,128)}) fusion(f32[1536]{0:T(1024)} %param.8, f32[1536]{0:T(1024)} %param.9, f32[1536,128]{1,0:T(8,128)} %param.6, f32[1536,128]{1,0:T(8,128)} %param.7, f32[1536]{0:T(1024)S(1)} %get-tuple-element.11, f32[1536]{0:T(1024)S(1)} %get-tuple-element.12), kind=kOutput, calls=%fused_computation.10 | convolution fusion | flops 3642749952 | bytes 11046912 | tf_op jit(solution)/shard_map/dot_general | solution.py:13
  24.3 34.7 %pmax.14 = f32[1536]{0:T(1024)S(1)} all-reduce(f32[1536]{0:T(1024)S(1)} %get-tuple-element.4), channel_id=1, replica_groups=mesh['row'=16,'col'=16] {'row'}, use_global_device_ids=true, to_apply=%region_3.0 | all-reduce | flops 1536 | bytes 12288 | tf_op jit(solution)/shard_map/pmax | solution.py:36
  59.0 34.3 %pmax.15 = f32[1536]{0:T(1024)S(1)} all-reduce(f32[1536]{0:T(1024)S(1)} %get-tuple-element.5), channel_id=1, replica_groups=mesh['row'=16,'col'=16] {'col'}, use_global_device_ids=true, to_apply=%region_7.0 | all-reduce | flops 1536 | bytes 12288 | tf_op jit(solution)/shard_map/pmax | solution.py:35
  93.4 6.7 %exponential_reduce_fusion.1 = (f32[1536]{0:T(1024)S(1)}, f32[1536]{0:T(1024)S(1)}) fusion(f32[1536,1536]{0,1:T(8,128)} %get-tuple-element.8, f32[1536]{0:T(1024)S(1)} %pmax.14, f32[1536]{0:T(1024)S(1)} %copy-done.2, f32[1536]{0:T(1024)S(1)} %pmax.15, f32[1536]{0:T(1024)S(1)} %copy-done.3), kind=kLoop, calls=%fused_computation.8 | loop fusion | flops 18871296 | bytes 9474048 | tf_op jit(solution)/shard_map/reduce_sum | solution.py:38
  100.1 23.5 %psum.57 = f32[1536]{0:T(1024)S(1)} all-reduce(f32[1536]{0:T(1024)S(1)} %get-tuple-element.3), channel_id=1, replica_groups=mesh['row'=16,'col'=16] {'col'}, use_global_device_ids=true, to_apply=%region_9.0 | all-reduce | flops 1536 | bytes 12288 | tf_op jit(solution)/shard_map/psum | solution.py:37
  123.6 12.1 %convolution_reduce_fusion.5 = f32[1536]{0:T(1024)S(1)} fusion(f32[1536,1]{0,1:T(1,128)S(1)} %reshape.36, f32[1536,1536]{0,1:T(8,128)} %get-tuple-element.8, f32[1536]{0:T(1024)S(1)} %log_add_fusion, f32[1536]{0:T(1024)S(1)} %copy-done.3), kind=kOutput, calls=%fused_computation.19 | convolution fusion | flops 35389440 | bytes 9461760 | tf_op jit(solution)/shard_map/dot_general | solution.py:28
  135.7 56.0 %all-reduce = (f32[1536]{0:T(1024)S(1)}, f32[1536]{0:T(1024)S(1)}) all-reduce(f32[1536]{0:T(1024)S(1)} %convolution_reduce_fusion.5, f32[1536]{0:T(1024)S(1)} %get-tuple-element.2), channel_id=1, replica_groups=mesh['row'=16,'col'=16] {'row'}, use_global_device_ids=true, to_apply=%region_10.0 | all-reduce | flops 3072 | bytes 24576 | tf_op jit(solution)/shard_map/psum | solution.py:48
  191.8 9.0 %convolution_reduce_fusion.4 = f32[1536]{0:T(1024)S(1)} fusion(f32[1536,1]{0,1:T(1,128)S(1)} %reshape.38, f32[1536,1536]{0,1:T(8,128)} %get-tuple-element.8, f32[1536]{0:T(1024)S(1)} %log_add_fusion.1, f32[1536]{0:T(1024)S(1)} %copy-done.2), kind=kOutput, calls=%fused_computation.18 | convolution fusion | flops 35389440 | bytes 9461760 | tf_op jit(solution)/shard_map/dot_general | solution.py:28
  200.8 38.1 %psum.59 = f32[1536]{0:T(1024)S(1)} all-reduce(f32[1536]{0:T(1024)S(1)} %convolution_reduce_fusion.4), channel_id=1, replica_groups=mesh['row'=16,'col'=16] {'col'}, use_global_device_ids=true, to_apply=%region_11.0 | all-reduce | flops 1536 | bytes 12288 | tf_op jit(solution)/shard_map/psum | solution.py:53
  238.9 11.3 %convolution_reduce_fusion.3 = f32[1536]{0:T(1024)S(1)} fusion(f32[1536,1]{0,1:T(1,128)S(1)} %reshape.40, f32[1536,1536]{0,1:T(8,128)} %get-tuple-element.8, f32[1536]{0:T(1024)S(1)} %log_add_fusion, f32[1536]{0:T(1024)S(1)} %copy-done.3), kind=kOutput, calls=%fused_computation.17 | convolution fusion | flops 35389440 | bytes 9461760 | tf_op jit(solution)/shard_map/dot_general | solution.py:28
  250.3 29.0 %psum.60 = f32[1536]{0:T(1024)S(1)} all-reduce(f32[1536]{0:T(1024)S(1)} %convolution_reduce_fusion.3), channel_id=1, replica_groups=mesh['row'=16,'col'=16] {'row'}, use_global_device_ids=true, to_apply=%region_12.0 | all-reduce | flops 1536 | bytes 12288 | tf_op jit(solution)/shard_map/psum | solution.py:48
  279.3 9.0 %convolution_reduce_fusion.2 = f32[1536]{0:T(1024)S(1)} fusion(f32[1536,1]{0,1:T(1,128)S(1)} %reshape.42, f32[1536,1536]{0,1:T(8,128)} %get-tuple-element.8, f32[1536]{0:T(1024)S(1)} %log_add_fusion.1, f32[1536]{0:T(1024)S(1)} %copy-done.2), kind=kOutput, calls=%fused_computation.16 | convolution fusion | flops 35389440 | bytes 9461760 | tf_op jit(solution)/shard_map/dot_general | solution.py:28
  288.4 31.2 %psum.61 = f32[1536]{0:T(1024)S(1)} all-reduce(f32[1536]{0:T(1024)S(1)} %convolution_reduce_fusion.2), channel_id=1, replica_groups=mesh['row'=16,'col'=16] {'col'}, use_global_device_ids=true, to_apply=%region_13.0 | all-reduce | flops 1536 | bytes 12288 | tf_op jit(solution)/shard_map/psum | solution.py:53
  319.6 11.3 %convolution_reduce_fusion.1 = f32[1536]{0:T(1024)S(1)} fusion(f32[1536,1]{0,1:T(1,128)S(1)} %reshape.44, f32[1536,1536]{0,1:T(8,128)} %get-tuple-element.8, f32[1536]{0:T(1024)S(1)} %log_add_fusion, f32[1536]{0:T(1024)S(1)} %copy-done.3), kind=kOutput, calls=%fused_computation.15 | convolution fusion | flops 35389440 | bytes 9461760 | tf_op jit(solution)/shard_map/dot_general | solution.py:28
  330.9 30.7 %psum.62 = f32[1536]{0:T(1024)S(1)} all-reduce(f32[1536]{0:T(1024)S(1)} %convolution_reduce_fusion.1), channel_id=1, replica_groups=mesh['row'=16,'col'=16] {'row'}, use_global_device_ids=true, to_apply=%region_14.0 | all-reduce | flops 1536 | bytes 12288 | tf_op jit(solution)/shard_map/psum | solution.py:48
  361.7 9.2 %convolution_reduce_fusion = f32[1536]{0:T(1024)S(1)} fusion(f32[1536,1]{0,1:T(1,128)S(1)} %reshape.46, f32[1536,1536]{0,1:T(8,128)} %get-tuple-element.8, f32[1536]{0:T(1024)S(1)} %log_add_fusion.1, f32[1536]{0:T(1024)S(1)} %copy-done.2), kind=kOutput, calls=%fused_computation.14 | convolution fusion | flops 35389440 | bytes 9461760 | tf_op jit(solution)/shard_map/dot_general | solution.py:28
  370.9 31.3 %psum.63 = f32[1536]{0:T(1024)S(1)} all-reduce(f32[1536]{0:T(1024)S(1)} %convolution_reduce_fusion), channel_id=1, replica_groups=mesh['row'=16,'col'=16] {'col'}, use_global_device_ids=true, to_apply=%region_15.0 | all-reduce | flops 1536 | bytes 12288 | tf_op jit(solution)/shard_map/psum | solution.py:53
  402.2 7.5 %fusion.2 = f32[1536]{0:T(1024)S(1)} fusion(f32[1536]{0:T(1024)S(1)} %sub.77, f32[1536]{0:T(1024)S(1)} %sub.78, f32[1536]{0:T(1024)S(1)} %log_add_fusion.1, f32[1536,1536]{0,1:T(8,128)} %get-tuple-element.8, f32[1536]{0:T(1024)S(1)} %copy-done.2, f32[1536]{0:T(1024)S(1)} %log_add_fusion, f32[1536]{0:T(1024)S(1)} %copy-done.3), kind=kLoop, calls=%fused_computation.20 | loop fusion | flops 23591424 | bytes 9480192 | tf_op jit(solution)/shard_map/reduce_sum | solution.py:63
  409.8 22.8 %convolution_subtract_fusion.3 = f32[1536,128]{1,0:T(8,128)} fusion(f32[1536,128]{1,0:T(8,128)S(1)} %copy-done, f32[1536]{0:T(1024)S(1)} %sub.77, f32[1536]{0:T(1024)S(1)} %sub.78, f32[1536,128]{1,0:T(8,128)S(1)} %copy-done.1, f32[1536]{0:T(1024)S(1)} %fusion.2, f32[1536,1536]{0,1:T(8,128)} %get-tuple-element.8, f32[1536]{0:T(1024)S(1)} %log_add_fusion.1, ...), kind=kOutput, calls=%fused_computation.13 | convolution fusion | flops 3645505536 | bytes 11839488 | tf_op jit(solution)/shard_map/dot_general | solution.py:28
  432.6 12.3 %fusion.3 = (f32[1536]{0:T(1024)S(1)}, f32[1536,1536]{0,1:T(8,128)S(1)}) fusion(f32[1536]{0:T(1024)S(1)} %log_add_fusion, f32[1536]{0:T(1024)S(1)} %copy-done.3, f32[1536]{0:T(1024)S(1)} %sub.78, f32[1536]{0:T(1024)S(1)} %log_add_fusion.1, f32[1536,128]{1,0:T(8,128)S(1)} %copy-done, f32[1536,128]{1,0:T(8,128)S(1)} %copy-done.1, ...), kind=kOutput, calls=%fused_computation.27 | convolution fusion | flops 3652188672 | bytes 11065344 | tf_op jit(solution)/shard_map/dot_general | solution.py:13
  445.0 16.0 %convolution_subtract_fusion.2 = f32[1536,128]{1,0:T(8,128)} fusion(f32[1536,1536]{0,1:T(8,128)S(1)} %get-tuple-element.10, f32[1536,128]{1,0:T(8,128)S(1)} %copy-done.1, f32[1536,128]{1,0:T(8,128)S(1)} %copy-done, f32[1536]{0:T(1024)S(1)} %get-tuple-element.9), kind=kOutput, calls=%fused_computation.12 | convolution fusion | flops 3624271872 | bytes 11802624 | tf_op jit(solution)/shard_map/dot_general | solution.py:28
  461.0 21.0 %reduce-scatter.3.cloned.1.call-done = f32[96,128]{1,0:T(8,128)} async-done(((f32[1536,128]{1,0:T(8,128)}), f32[96,128]{1,0:T(8,128)}) %reduce-scatter.3.cloned.1.call-update) | async-done | bytes 49168 | tf_op jit(solution)/shard_map/reduce_scatter | solution.py:62
  482.0 81.8 %reduce-scatter.5.cloned.1.call-done = f32[96,128]{1,0:T(8,128)} async-done(((f32[1536,128]{1,0:T(8,128)}), f32[96,128]{1,0:T(8,128)}) %reduce-scatter.5.cloned.1.call-update) | async-done | bytes 49168 | tf_op jit(solution)/shard_map/reduce_scatter | solution.py:76
  (32 shorter events, 2.3 us)
Async XLA Ops:
  7.2 474.9 %reduce-scatter.3.cloned.1.call-start = ((), (), s32[]{:S(2)}) async-start(), calls=%async_computation.2 | async-start | bytes 835584 | tf_op jit(solution)/shard_map/reduce_scatter | solution.py:62
  10.8 82.6 %copy-start.2 = (f32[1536]{0:T(1024)S(1)}, f32[1536]{0:T(1024)}, u32[]{:S(2)}) copy-start(f32[1536]{0:T(1024)} %param.8) | copy-start | bytes 18436
  10.8 82.6 %copy-start.3 = (f32[1536]{0:T(1024)S(1)}, f32[1536]{0:T(1024)}, u32[]{:S(2)}) copy-start(f32[1536]{0:T(1024)} %param.9) | copy-start | bytes 18436
  93.4 98.4 %copy-start.5 = (f32[1536]{0:T(1024)S(1)}, f32[1536]{0:T(1024)}, u32[]{:S(2)}) copy-start(f32[1536]{0:T(1024)} %param.11) | copy-start | bytes 18436
  123.6 115.3 %copy-start.4 = (f32[1536]{0:T(1024)S(1)}, f32[1536]{0:T(1024)}, u32[]{:S(2)}) copy-start(f32[1536]{0:T(1024)} %param.10) | copy-start | bytes 18436
  361.7 48.0 %copy-start = (f32[1536,128]{1,0:T(8,128)S(1)}, f32[1536,128]{1,0:T(8,128)}, u32[]{:S(2)}) copy-start(f32[1536,128]{1,0:T(8,128)} %param.7) | copy-start | bytes 2359300
  361.7 48.0 %copy-start.1 = (f32[1536,128]{1,0:T(8,128)S(1)}, f32[1536,128]{1,0:T(8,128)}, u32[]{:S(2)}) copy-start(f32[1536,128]{1,0:T(8,128)} %param.6) | copy-start | bytes 2359300
  432.6 131.3 %reduce-scatter.5.cloned.1.call-start = ((), (), s32[]{:S(2)}) async-start(), calls=%async_computation.3 | async-start | bytes 835584 | tf_op jit(solution)/shard_map/reduce_scatter | solution.py:76
Sparse Core Ops, SparseCore 0:
  432.7 49.2 reduce-scatter.2
  486.5 77.3 reduce-scatter.4
where the time goes:
time: 580 us; the launch traced here: 571 us
  blocking collectives  309 us (53%)
  matrix products  127 us (22%)
  waiting for transfers between devices  103 us (18%)
  other arithmetic  17.1 us (3%)
  between operations  14.8 us (3%)
    psum x3, blocking collectives, shards(): target_adj = target_cot - lax.psum(target_push, 'row')  116 us
    reduce_scatter x2, waiting for transfers between devices, shards(): lax.psum_scatter(block * jnp.sum(weight, axis=1)[:, None] - hot_dot(weigh...  103 us
    dot_general x8, matrix products, hot_dot(): jnp.dot(left, right, precision=lax.Precision.HIGHEST, preferred_element_t...  101 us
    psum x3, blocking collectives, shards(): source_adj = source_cot - lax.psum(source_push, 'col')  101 us
    pmax x1, blocking collectives, shards(): col_peak = lax.pmax(jnp.max(col_logits, axis=0), 'row')  34.7 us
    pmax x1, blocking collectives, shards(): row_peak = lax.pmax(jnp.max(row_logits, axis=1), 'col')  34.3 us
    dot_general x2, matrix products, pair_distance(): lax.dot_general(query, others, (((1,), (1,)), ((), ())), precision=lax.Pr...  25.8 us
    psum x1, blocking collectives, shards(): lax.psum(jnp.sum(jnp.exp(row_logits - row_peak[:, None]), axis=1), 'col')  23.5 us
  transfers between devices with their start and end apart: 2, of which 2 were waited for; matrix products, arithmetic and copies ran while one was open for 5% of the time, Pallas kernels for 0%

commit v1 on v0

v1 whole, which is shorter than its diff:
```python
import functools

import jax
import jax.numpy as jnp
from jax import lax
from jax.experimental import pallas as pl
from jax.experimental.pallas import tpu as pltpu
from jax.sharding import PartitionSpec as P

MESH = pl.DeviceIdType.MESH
F32 = jnp.float32
BF16 = jnp.bfloat16
LOG2E = 1.4426950408889634
D = 128
NT = (((1,), (1,)), ((), ()))
NN = (((1,), (0,)), ((), ()))


def mm(left, right, dims):
    return lax.dot_general(left, right, dims, preferred_element_type=F32)


def split(value):
    high = value.astype(BF16)
    return high, (value - high.astype(F32)).astype(BF16)


def column(row):
    return jnp.broadcast_to(row, (128, 128)).T


def kernel(
    nr, nc, cb, lane_chunk,
    x_ref, y_ref, f_ref, g_ref, sc_ref, tc_ref, gs_ref, gt_ref,
    xc, yc, rt, s, rt_hi, rt_lo, s_hi, s_lo, xt, yt, xt2, yt2, scaled,
    peak, coef, send, recv, ssem, rsem,
    ry, ry_pair, ry_send, ry_recv, sx, sx_recv,
    zp, zp_pair, zp_send, zp_recv, tp, tp_recv, cols,
    bulk_s, bulk_r, late_s, late_r,
):
    size = x_ref.shape[0]
    groups = size // 128
    chunks = size // lane_chunk
    wide = lane_chunk // 128
    sub_r, sub_c = size // nr, size // nc
    r, c = lax.axis_index("row"), lax.axis_index("col")
    z, h = c // 2, lax.rem(c, 2)

    barrier = pltpu.get_barrier_semaphore()
    for d in range(1, nr):
        pl.semaphore_signal(barrier, inc=1, device_id=(lax.rem(r + d, nr), c), device_id_type=MESH)
    for d in range(1, nc):
        pl.semaphore_signal(barrier, inc=1, device_id=(r, lax.rem(c + d, nc)), device_id_type=MESH)

    lane = lax.broadcasted_iota(jnp.int32, (128, 128), 1)

    def prepare(k, _):
        rows = pl.ds(pl.multiple_of(k * 128, 128), 128)
        for ref, pot, cat, scale, first, order in (
            (x_ref, f_ref, xc, 2.0 * LOG2E, 0, (0, 1, 0)),
            (y_ref, g_ref, yc, 1.0, 3, (0, 0, 1)),
        ):
            tile = ref[rows, :]
            parts = split(tile * scale)
            for slot, which in enumerate(order):
                cat[rows, slot * D:(slot + 1) * D] = parts[which]
            norm = jnp.sum(tile * tile, axis=1, keepdims=True)
            offset = LOG2E * (2.0 * column(pot[pl.ds(k, 1), :]) - norm)
            one = offset.astype(BF16).astype(F32)
            two = (offset - one).astype(BF16).astype(F32)
            three = offset - one - two
            extra = jnp.where(lane < 6, 1.0, 0.0)
            for place, piece in enumerate((one, two, three)):
                extra = jnp.where(lane == first + place, piece, extra)
            cat[rows, 3 * D:] = extra.astype(BF16)
        return 0

    lax.fori_loop(0, groups, prepare, 0)

    def soften(left, right, out, peak_slot, round_slot):
        tall = 256 if size % 256 == 0 else 128

        def one(k, _):
            lanes = pl.ds(pl.multiple_of(k * lane_chunk, lane_chunk), lane_chunk)
            rhs = right[lanes, :]

            def logits(q, top):
                rows = pl.ds(pl.multiple_of(q * tall, tall), tall)
                tile = mm(left[rows, :], rhs, NT)
                out[rows, lanes] = tile
                return jnp.maximum(top, jnp.max(tile.reshape(tall // 8, 8, lane_chunk), axis=0))

            top = lax.fori_loop(0, size // tall, logits, jnp.full((8, lane_chunk), -jnp.inf, F32), unroll=True)
            top = jnp.max(top, axis=0, keepdims=True)

            def weights(q, total):
                rows = pl.ds(pl.multiple_of(q * 64, 64), 64)
                tile = jnp.exp2(out[rows, lanes] - top)
                out[rows, lanes] = tile
                return total + jnp.sum(tile.reshape(8, 8, lane_chunk), axis=0)

            total = lax.fori_loop(0, size // 64, weights, jnp.zeros((8, lane_chunk), F32))
            total = jnp.sum(total, axis=0, keepdims=True)
            local = top + LOG2E * jnp.log(total)
            for w in range(wide):
                peak[peak_slot, pl.ds(k * wide + w, 1), :] = top[:, w * 128:(w + 1) * 128]
                send[round_slot, pl.ds(k * wide + w, 1), :] = local[:, w * 128:(w + 1) * 128]
            return 0

        lax.fori_loop(0, chunks, one, 0)

    def exchange(slot, along_row):
        n = nr if along_row else nc
        order = sorted(range(1, n), key=lambda d: -min(d, n - d))
        for d in order:
            device = (lax.rem(r + d, n), c) if along_row else (r, lax.rem(c + d, n))
            pltpu.make_async_remote_copy(
                send.at[slot], recv.at[slot, d - 1], ssem.at[slot], rsem.at[slot],
                device_id=device, device_id_type=MESH,
            ).start()

    def wait_bytes(ref, sem):
        pltpu.make_async_copy(ref, ref, sem).wait()

    def arrived(slot, n):
        wait_bytes(recv.at[slot, pl.ds(0, n - 1)], rsem.at[slot])

    def total_of(slot, n):
        total = send[slot]
        for d in range(n - 1):
            total = total + recv[slot, d]
        return total

    def norm_scale(slot, n, peak_slot):
        top = send[slot]
        for d in range(n - 1):
            top = jnp.maximum(top, recv[slot, d])
        total = jnp.exp2(send[slot] - top)
        for d in range(n - 1):
            total = total + jnp.exp2(recv[slot, d] - top)
        return jnp.exp2(peak[peak_slot] - top - LOG2E * jnp.log(total))

    def matvec(matrix, slot):
        def one(k, _):
            rows = pl.ds(pl.multiple_of(k * 128, 128), 128)
            acc = matrix[rows, 0:128] * coef[0:1, :]
            for q in range(1, groups):
                acc = acc + matrix[rows, q * 128:(q + 1) * 128] * coef[q:q + 1, :]
            send[slot, pl.ds(k, 1), :] = jnp.sum(acc.T, axis=0, keepdims=True)
            return 0

        lax.fori_loop(0, groups, one, 0)

    def halves(matrix, high, low):
        def one(k, _):
            rows = pl.ds(pl.multiple_of(k * 32, 32), 32)
            high[rows, :], low[rows, :] = split(matrix[rows, :])
            return 0

        lax.fori_loop(0, size // 32, one, 0)

    def turned(ref, out, out2):
        for k in range(groups):
            lanes = slice(k * 128, (k + 1) * 128)
            tile = ref[lanes, :].T
            out[:, lanes] = tile
            out2[0:D, lanes], out2[D:2 * D, lanes] = split(tile)

    def early(points2, high, low, scale, out):
        for k in range(chunks):
            lanes = slice(k * lane_chunk, (k + 1) * lane_chunk)
            both = mm(points2[...], high[:, lanes], NN)
            tile = both[0:D] + both[D:2 * D] + mm(points2[0:D, :], low[:, lanes], NN)
            for w in range(wide):
                group = k * wide + w
                block = tile[:, w * 128:(w + 1) * 128] * scale[group:group + 1, :]
                out[group * 128:(group + 1) * 128, :] = block.T

    def scale_points(points):
        for k in range(groups):
            lanes = slice(k * 128, (k + 1) * 128)
            scaled[0:D, lanes], scaled[D:2 * D, lanes] = split(points[:, lanes] * coef[k:k + 1, :])

    half = cb // 2
    ch_c, ch_r = nc // cb, nr // cb

    def offsets(n):
        return sorted(range(n), key=lambda o: -min(o, n - o))

    def z_dest(o, t):
        return lax.rem(z // half + o, ch_c) * half + lax.rem(z + t, half)

    def r_dest(o, t):
        return lax.rem(r // cb + o, ch_r) * cb + lax.rem(r + t, cb)

    z_list = [(o, t) for o in offsets(ch_c) for t in reversed(range(half))]
    r_list = [(o, t) for o in offsets(ch_r) for t in reversed(range(cb))]

    def block(index, rows):
        return pl.ds(pl.multiple_of(index * rows, 8), rows)

    def to_partner(source, pair, slot, o, t, s_sem, r_sem):
        pltpu.make_async_remote_copy(
            source.at[block(z_dest(o, t) * 2 + 1 - h, sub_c)], pair.at[slot], s_sem, r_sem,
            device_id=(r, z * 2 + 1 - h), device_id_type=MESH,
        ).start()

    def along_z(out, inbox, slot, o, t, s_sem, r_sem):
        pltpu.make_async_remote_copy(
            out.at[slot], inbox.at[slot], s_sem, r_sem,
            device_id=(r, z_dest(o, t) * 2 + h), device_id_type=MESH,
        ).start()

    def along_r(source, inbox, slot, o, t, s_sem, r_sem):
        pltpu.make_async_remote_copy(
            source.at[block(r_dest(o, t), sub_r)], inbox.at[slot], s_sem, r_sem,
            device_id=(r_dest(o, t), c), device_id_type=MESH,
        ).start()

    nz = nc // 2

    soften(yc, xc, rt, 0, 0)
    pl.semaphore_wait(barrier, nr + nc - 2)
    exchange(0, False)
    soften(xc, yc, s, 1, 1)
    exchange(1, True)
    turned(y_ref, yt, yt2)
    turned(x_ref, xt, xt2)
    arrived(0, nc)
    rho = norm_scale(0, nc, 0)

    coef[...] = rho * sc_ref[...]
    matvec(rt, 2)
    exchange(2, True)
    halves(rt, rt_hi, rt_lo)
    early(yt2, rt_hi, rt_lo, rho, ry)
    for slot, (o, t) in enumerate(z_list):
        to_partner(ry, ry_pair, slot, o, t, bulk_s.at[0], bulk_r.at[0])
    arrived(1, nr)
    sigma = norm_scale(1, nr, 1)
    arrived(2, nr)
    target_adj = tc_ref[...] - total_of(2, nr)

    coef[...] = sigma * target_adj
    matvec(s, 3)
    exchange(3, False)
    halves(s, s_hi, s_lo)
    wait_bytes(ry_pair, bulk_r.at[0])
    for slot, (o, t) in enumerate(z_list):
        ry_send[slot] = ry[block(z_dest(o, t) * 2 + h, sub_c), :] + ry_pair[slot]
    arrived(3, nc)
    source_adj = sc_ref[...] - total_of(3, nc)

    coef[...] = rho * source_adj
    matvec(rt, 4)
    exchange(4, True)
    cut = nz // 2
    for slot in range(cut):
        along_z(ry_send, ry_recv, slot, *z_list[slot], bulk_s.at[1], bulk_r.at[1])
    early(xt2, s_hi, s_lo, sigma, sx)
    arrived(4, nr)
    target_adj = tc_ref[...] - total_of(4, nr)

    coef[...] = sigma * target_adj
    matvec(s, 5)
    exchange(5, False)
    for slot, (o, t) in enumerate(r_list[:-1]):
        along_r(sx, sx_recv, slot, o, t, bulk_s.at[3], bulk_r.at[3])
    arrived(5, nc)
    source_adj = sc_ref[...] - total_of(5, nc)

    coef[...] = rho * source_adj
    matvec(rt, 6)
    exchange(6, True)
    for slot in range(cut, nz - 1):
        along_z(ry_send, ry_recv, slot, *z_list[slot], bulk_s.at[2], bulk_r.at[2])
    arrived(6, nr)
    target_adj = tc_ref[...] - total_of(6, nr)

    coef[...] = sigma * target_adj
    matvec(s, 7)
    exchange(7, False)
    scale_points(yt)
    tall_c = cb * sub_c

    def z_forward(n):
        wait_bytes(zp_pair.at[pl.ds(n * half, half)], late_r.at[n])
        for slot in range(n * half, (n + 1) * half):
            o, t = z_list[slot]
            zp_send[slot] = zp[block(z_dest(o, t) * 2 + h, sub_c), :] + zp_pair[slot]
            if slot < nz - 1:
                along_z(zp_send, zp_recv, slot, o, t, late_s.at[ch_c], late_r.at[ch_c])

    for n in range(ch_c):
        rows = block(lax.rem(z // half + z_list[n * half][0], ch_c), tall_c)
        both = mm(s_hi[rows, :], scaled[...], NT)
        zp[rows, :] = both[:, 0:D] + both[:, D:2 * D] + mm(s_lo[rows, :], scaled[0:D, :], NT)
        for slot in range(n * half, (n + 1) * half):
            to_partner(zp, zp_pair, slot, *z_list[slot], late_s.at[n], late_r.at[n])
        if n:
            z_forward(n - 1)
    z_forward(ch_c - 1)

    arrived(7, nc)
    source_adj = sc_ref[...] - total_of(7, nc)

    coef[...] = rho * source_adj
    scale_points(xt)
    tall_r = cb * sub_r
    for n in range(ch_r):
        rows = block(lax.rem(r // cb + r_list[n * cb][0], ch_r), tall_r)
        both = mm(rt_hi[rows, :], scaled[...], NT)
        moved = both[:, 0:D] + both[:, D:2 * D] + mm(rt_lo[rows, :], scaled[0:D, :], NT)
        acc = rt[rows, 0:128] * coef[0:1, :]
        for q in range(1, groups):
            acc = acc + rt[rows, q * 128:(q + 1) * 128] * coef[q:q + 1, :]
        tp[rows, :] = y_ref[rows, :] * jnp.sum(acc, axis=1, keepdims=True) - moved
        for slot in range(n * cb, (n + 1) * cb):
            if slot < nr - 1:
                along_r(tp, tp_recv, slot, *r_list[slot], late_s.at[ch_c + 1], late_r.at[ch_c + 1])

    for k in range(groups):
        rows = slice(k * 128, (k + 1) * 128)
        cols[0, rows, :] = column(sc_ref[k:k + 1, :])
        cols[1, rows, :] = column(source_adj[k:k + 1, :])
        cols[2, rows, :] = column(target_adj[k:k + 1, :])

    own_c, own_r = block(c, sub_c), block(r, sub_r)
    wait_bytes(ry_recv.at[pl.ds(0, cut)], bulk_r.at[1])
    wait_bytes(ry_recv.at[pl.ds(cut, nz - 1 - cut)], bulk_r.at[2])
    moved = ry_send[nz - 1]
    for slot in range(nz - 1):
        moved = moved + ry_recv[slot]
    wait_bytes(sx_recv, bulk_r.at[3])
    other = sx[own_r, :]
    for slot in range(nr - 1):
        other = other + sx_recv[slot]
    wait_bytes(zp_recv, late_r.at[ch_c])
    late = zp_send[nz - 1]
    for slot in range(nz - 1):
        late = late + zp_recv[slot]
    gs_ref[...] = x_ref[own_c, :] * cols[0, own_c, :] - cols[1, own_c, :] * moved - late
    wait_bytes(tp_recv, late_r.at[ch_c + 1])
    late = tp[own_r, :]
    for slot in range(nr - 1):
        late = late + tp_recv[slot]
    gt_ref[...] = cols[2, own_r, :] * (y_ref[own_r, :] - other) + late

    for slot, n in enumerate((nc, nr, nr, nc, nr, nc, nr, nc)):
        wait_bytes(recv.at[slot, pl.ds(0, n - 1)], ssem.at[slot])
    wait_bytes(ry_pair, bulk_s.at[0])
    wait_bytes(ry_recv.at[pl.ds(0, cut)], bulk_s.at[1])
    wait_bytes(ry_recv.at[pl.ds(cut, nz - 1 - cut)], bulk_s.at[2])
    wait_bytes(sx_recv, bulk_s.at[3])
    for n in range(ch_c):
        wait_bytes(zp_pair.at[pl.ds(n * half, half)], late_s.at[n])
    wait_bytes(zp_recv, late_s.at[ch_c])
    wait_bytes(tp_recv, late_s.at[ch_c + 1])


def shards(nr, nc, cb, lane_chunk, x, y, f, g, sc, tc):
    size = x.shape[0]
    groups = size // 128
    sub_r, sub_c = size // nr, size // nc
    vectors = [v.reshape(groups, 128) for v in (f, g, sc, tc)]
    vmem = pl.BlockSpec(memory_space=pltpu.VMEM)
    peers = max(nr, nc) - 1
    nz = nc // 2
    square = (size, size)
    return pl.pallas_call(
        functools.partial(kernel, nr, nc, cb, lane_chunk),
        out_shape=(
            jax.ShapeDtypeStruct((sub_c, D), F32),
            jax.ShapeDtypeStruct((sub_r, D), F32),
        ),
        in_specs=[vmem] * 6,
        out_specs=(vmem, vmem),
        scratch_shapes=[
            pltpu.VMEM((size, 4 * D), BF16),
            pltpu.VMEM((size, 4 * D), BF16),
            pltpu.VMEM(square, F32),
            pltpu.VMEM(square, F32),
            pltpu.VMEM(square, BF16),
            pltpu.VMEM(square, BF16),
            pltpu.VMEM(square, BF16),
            pltpu.VMEM(square, BF16),
            pltpu.VMEM((D, size), F32),
            pltpu.VMEM((D, size), F32),
            pltpu.VMEM((2 * D, size), BF16),
            pltpu.VMEM((2 * D, size), BF16),
            pltpu.VMEM((2 * D, size), BF16),
            pltpu.VMEM((2, groups, 128), F32),
            pltpu.VMEM((groups, 128), F32),
            pltpu.VMEM((8, groups, 128), F32),
            pltpu.VMEM((8, peers, groups, 128), F32),
            pltpu.SemaphoreType.DMA((8,)),
            pltpu.SemaphoreType.DMA((8,)),
            pltpu.VMEM((size, D), F32),
            pltpu.VMEM((nz, sub_c, D), F32),
            pltpu.VMEM((nz, sub_c, D), F32),
            pltpu.VMEM((nz - 1, sub_c, D), F32),
            pltpu.VMEM((size, D), F32),
            pltpu.VMEM((nr - 1, sub_r, D), F32),
            pltpu.VMEM((size, D), F32),
            pltpu.VMEM((nz, sub_c, D), F32),
            pltpu.VMEM((nz, sub_c, D), F32),
            pltpu.VMEM((nz - 1, sub_c, D), F32),
            pltpu.VMEM((size, D), F32),
            pltpu.VMEM((nr - 1, sub_r, D), F32),
            pltpu.VMEM((3, size, D), F32),
            pltpu.SemaphoreType.DMA((4,)),
            pltpu.SemaphoreType.DMA((4,)),
            pltpu.SemaphoreType.DMA((nc // cb + 2,)),
            pltpu.SemaphoreType.DMA((nc // cb + 2,)),
        ],
        compiler_params=pltpu.CompilerParams(
            collective_id=0, has_side_effects=True, vmem_limit_bytes=62 << 20
        ),
    )(x, y, *vectors)


def solution(mesh, cb=4, lane_chunk=256):
    in_specs = (P("row", None), P("col", None), P("row"), P("col"), P("row"), P("col"))
    out_specs = (P(("row", "col"), None), P(("col", "row"), None))
    body = functools.partial(shards, mesh.shape["row"], mesh.shape["col"], cb, lane_chunk)
    return jax.shard_map(body, mesh=mesh, in_specs=in_specs, out_specs=out_specs, check_vma=False)
```

time: 580 us -> 82.8 us (0.14); the launches traced: 571 us -> 82.6 us
  blocking collectives: 309 us -> 0 us
  matrix products: 127 us -> 0 us
  waiting for transfers between devices: 103 us -> 0 us
  Pallas kernels: 0 us -> 79.9 us
  other arithmetic: 17.1 us -> 0 us
  between operations: 14.8 us -> 0.65 us
    psum x7 -> x0, blocking collectives: 240 us -> none  [the longest x3 116 us: shards(): target_adj = target_cot - lax.psum(target_push, 'row')]
    dot_general x10 -> x0, matrix products: 127 us -> none  [the longest x8 101 us: hot_dot(): jnp.dot(left, right, precision=lax.Precision.HIGHEST, preferred_element_t...]
    reduce_scatter x2 -> x0, waiting for transfers between devices: 103 us -> none  [shards(): lax.psum_scatter(block * jnp.sum(weight, axis=1)[:, None] - hot_dot(weigh...]
    pallas_call x0 -> x1, Pallas kernels: none -> 79.9 us  [shards(): pl.pallas_call(functools.partial(kernel, nr, nc, cb, lane_chunk), out_sha...]
    pmax x2 -> x0, blocking collectives: 69 us -> none  [the longest x1 34.7 us: shards(): col_peak = lax.pmax(jnp.max(col_logits, axis=0), 'row')]
    reduce_sum x4 -> x0, other arithmetic: 17 us -> none  [the longest x1 7.52 us: shards(): jnp.sum(weight, axis=1)[:, None]]
  transfers between devices with their start and end apart: 2 -> 0, of which waited for: 2 -> 0; matrix products, arithmetic and copies ran while one was open for 5% -> 0% of each run, Pallas kernels for 0% -> 0%
where the time goes in v1:
time: 82.8 us; the launch traced here: 82.6 us
  Pallas kernels  79.9 us (96%)
  local copies, waits for them, and re-layouts  2.06 us (2%)
    pallas_call x1, Pallas kernels, shards(): pl.pallas_call(functools.partial(kernel, nr, nc, cb, lane_chunk), out_sha...  79.9 us
    unnamed x4, local copies, waits for them, and re-layouts  2.06 us

profile of v1, /device:TPU:1, one launch (start us, length us, event | category | flops | bytes accessed | tf_op | source)
XLA Modules:
  0.0 82.6 jit_solution(16043883139759249218)
XLA Ops:
  0.6 79.9 %shard_map.77 = (f32[96,128]{1,0:T(8,128)}, f32[96,128]{1,0:T(8,128)}) custom-call(f32[1536,128]{1,0:T(8,128)} %x_ref.1, f32[1536,128]{1,0:T(8,128)} %y_ref.1, f32[12,128]{1,0:T(8,128)} %bitcast.4, f32[12,128]{1,0:T(8,128)} %bitcast.5, f32[12,128]{1,0:T(8,128)} %bitcast.6, f32[12,128]{1,0:T(8,128)} %bitcast.7), custom_call_target="tpu_custom_call" | custom-call | tf_op jit(solution)/shard_map/pallas_call | solution.py:370
  80.5 0.0 copy-start
  80.5 1.4 %copy.10 = f32[96,128]{1,0:T(8,128)} copy(f32[96,128]{1,0:T(8,128)} %get-tuple-element.4) | data formatting | bytes 98304
  82.0 0.0 copy-done
  82.0 0.6 copy.11
Async XLA Ops:
  80.5 1.4 %copy-start = (f32[96,128]{1,0:T(8,128)S(1)}, f32[96,128]{1,0:T(8,128)}, u32[]{:S(2)}) copy-start(f32[96,128]{1,0:T(8,128)} %get-tuple-element.5) | copy-start | bytes 147460

commit v2 on v1

--- a/solution.py
+++ b/solution.py
@@ -30,11 +30,11 @@
 
 
 def kernel(
-    nr, nc, cb, lane_chunk,
+    nr, nc, cb, lane_chunk, pieces,
     x_ref, y_ref, f_ref, g_ref, sc_ref, tc_ref, gs_ref, gt_ref,
     xc, yc, rt, s, rt_hi, rt_lo, s_hi, s_lo, xt, yt, xt2, yt2, scaled,
     peak, coef, send, recv, ssem, rsem,
-    ry, ry_pair, ry_send, ry_recv, sx, sx_recv,
+    ry, ry_pair, ry_send, ry_recv, sx,
     zp, zp_pair, zp_send, zp_recv, tp, tp_recv, cols,
     bulk_s, bulk_r, late_s, late_r,
 ):
@@ -42,6 +42,7 @@
     groups = size // 128
     chunks = size // lane_chunk
     wide = lane_chunk // 128
+    per = groups // pieces
     sub_r, sub_c = size // nr, size // nc
     r, c = lax.axis_index("row"), lax.axis_index("col")
     z, h = c // 2, lax.rem(c, 2)
@@ -54,8 +55,8 @@
 
     lane = lax.broadcasted_iota(jnp.int32, (128, 128), 1)
 
-    def prepare(k, _):
-        rows = pl.ds(pl.multiple_of(k * 128, 128), 128)
+    def prepare(k):
+        rows = slice(k * 128, (k + 1) * 128)
         for ref, pot, cat, scale, first, order in (
             (x_ref, f_ref, xc, 2.0 * LOG2E, 0, (0, 1, 0)),
             (y_ref, g_ref, yc, 1.0, 3, (0, 0, 1)),
@@ -65,7 +66,7 @@
             for slot, which in enumerate(order):
                 cat[rows, slot * D:(slot + 1) * D] = parts[which]
             norm = jnp.sum(tile * tile, axis=1, keepdims=True)
-            offset = LOG2E * (2.0 * column(pot[pl.ds(k, 1), :]) - norm)
+            offset = LOG2E * (2.0 * column(pot[k:k + 1, :]) - norm)
             one = offset.astype(BF16).astype(F32)
             two = (offset - one).astype(BF16).astype(F32)
             three = offset - one - two
@@ -73,50 +74,50 @@
             for place, piece in enumerate((one, two, three)):
                 extra = jnp.where(lane == first + place, piece, extra)
             cat[rows, 3 * D:] = extra.astype(BF16)
-        return 0
-
-    lax.fori_loop(0, groups, prepare, 0)
-
-    def soften(left, right, out, peak_slot, round_slot):
+
+    for k in range(groups):
+        prepare(k)
+
+    def soften(left, right, out, peak_slot, round_slot, along_row):
         tall = 256 if size % 256 == 0 else 128
-
-        def one(k, _):
-            lanes = pl.ds(pl.multiple_of(k * lane_chunk, lane_chunk), lane_chunk)
-            rhs = right[lanes, :]
-
-            def logits(q, top):
-                rows = pl.ds(pl.multiple_of(q * tall, tall), tall)
-                tile = mm(left[rows, :], rhs, NT)
-                out[rows, lanes] = tile
-                return jnp.maximum(top, jnp.max(tile.reshape(tall // 8, 8, lane_chunk), axis=0))
-
-            top = lax.fori_loop(0, size // tall, logits, jnp.full((8, lane_chunk), -jnp.inf, F32), unroll=True)
-            top = jnp.max(top, axis=0, keepdims=True)
-
-            def weights(q, total):
-                rows = pl.ds(pl.multiple_of(q * 64, 64), 64)
-                tile = jnp.exp2(out[rows, lanes] - top)
-                out[rows, lanes] = tile
-                return total + jnp.sum(tile.reshape(8, 8, lane_chunk), axis=0)
-
-            total = lax.fori_loop(0, size // 64, weights, jnp.zeros((8, lane_chunk), F32))
-            total = jnp.sum(total, axis=0, keepdims=True)
-            local = top + LOG2E * jnp.log(total)
-            for w in range(wide):
-                peak[peak_slot, pl.ds(k * wide + w, 1), :] = top[:, w * 128:(w + 1) * 128]
-                send[round_slot, pl.ds(k * wide + w, 1), :] = local[:, w * 128:(w + 1) * 128]
-            return 0
-
-        lax.fori_loop(0, chunks, one, 0)
-
-    def exchange(slot, along_row):
+        tops = []
+        for k in range(chunks + 1):
+            top = jnp.full((8, lane_chunk), -jnp.inf, F32)
+            total = jnp.zeros((8, lane_chunk), F32)
+            ahead = slice(k * lane_chunk, (k + 1) * lane_chunk)
+            lanes = slice((k - 1) * lane_chunk, k * lane_chunk)
+            for q in range(size // tall):
+                rows = slice(q * tall, (q + 1) * tall)
+                if k < chunks:
+                    tile = mm(left[rows, :], right[ahead, :], NT)
+                    out[rows, ahead] = tile
+                    top = jnp.maximum(top, jnp.max(tile.reshape(tall // 8, 8, lane_chunk), axis=0))
+                if k:
+                    tile = jnp.exp2(out[rows, lanes] - tops[k - 1])
+                    out[rows, lanes] = tile
+                    total = total + jnp.sum(tile.reshape(tall // 8, 8, lane_chunk), axis=0)
+            if k < chunks:
+                tops.append(jnp.max(top, axis=0, keepdims=True))
+            if k:
+                total = jnp.sum(total, axis=0, keepdims=True)
+                local = tops[k - 1] + LOG2E * jnp.log(total)
+                for w in range(wide):
+                    group, part = (k - 1) * wide + w, slice(w * 128, (w + 1) * 128)
+                    peak[peak_slot, group:group + 1, :] = tops[k - 1][:, part]
+                    send[round_slot, group:group + 1, :] = local[:, part]
+                    if (group + 1) % per == 0:
+                        if group + 1 == per and not along_row:
+                            pl.semaphore_wait(barrier, nr + nc - 2)
+                        exchange(round_slot, along_row, group + 1 - per)
+
+    def exchange(slot, along_row, first):
         n = nr if along_row else nc
         order = sorted(range(1, n), key=lambda d: -min(d, n - d))
         for d in order:
             device = (lax.rem(r + d, n), c) if along_row else (r, lax.rem(c + d, n))
             pltpu.make_async_remote_copy(
-                send.at[slot], recv.at[slot, d - 1], ssem.at[slot], rsem.at[slot],
-                device_id=device, device_id_type=MESH,
+                send.at[slot, pl.ds(first, per)], recv.at[slot, d - 1, pl.ds(first, per)],
+                ssem.at[slot], rsem.at[slot], device_id=device, device_id_type=MESH,
             ).start()
 
     def wait_bytes(ref, sem):
@@ -140,16 +141,15 @@
             total = total + jnp.exp2(recv[slot, d] - top)
         return jnp.exp2(peak[peak_slot] - top - LOG2E * jnp.log(total))
 
-    def matvec(matrix, slot):
-        def one(k, _):
-            rows = pl.ds(pl.multiple_of(k * 128, 128), 128)
+    def push(matrix, slot, along_row):
+        for k in range(groups):
+            rows = slice(k * 128, (k + 1) * 128)
             acc = matrix[rows, 0:128] * coef[0:1, :]
             for q in range(1, groups):
                 acc = acc + matrix[rows, q * 128:(q + 1) * 128] * coef[q:q + 1, :]
-            send[slot, pl.ds(k, 1), :] = jnp.sum(acc.T, axis=0, keepdims=True)
-            return 0
-
-        lax.fori_loop(0, groups, one, 0)
+            send[slot, k:k + 1, :] = jnp.sum(acc.T, axis=0, keepdims=True)
+            if (k + 1) % per == 0:
+                exchange(slot, along_row, k + 1 - per)
 
     def halves(matrix, high, low):
         def one(k, _):
@@ -176,6 +176,10 @@
                 block = tile[:, w * 128:(w + 1) * 128] * scale[group:group + 1, :]
                 out[group * 128:(group + 1) * 128, :] = block.T
 
+    def fill_column(slot, rows_of):
+        for k in range(groups):
+            cols[slot, k * 128:(k + 1) * 128, :] = column(rows_of[k:k + 1, :])
+
     def scale_points(points):
         for k in range(groups):
             lanes = slice(k * 128, (k + 1) * 128)
@@ -219,19 +223,15 @@
 
     nz = nc // 2
 
-    soften(yc, xc, rt, 0, 0)
-    pl.semaphore_wait(barrier, nr + nc - 2)
-    exchange(0, False)
-    soften(xc, yc, s, 1, 1)
-    exchange(1, True)
+    soften(yc, xc, rt, 0, 0, False)
+    soften(xc, yc, s, 1, 1, True)
     turned(y_ref, yt, yt2)
     turned(x_ref, xt, xt2)
     arrived(0, nc)
     rho = norm_scale(0, nc, 0)
 
     coef[...] = rho * sc_ref[...]
-    matvec(rt, 2)
-    exchange(2, True)
+    push(rt, 2, True)
     halves(rt, rt_hi, rt_lo)
     early(yt2, rt_hi, rt_lo, rho, ry)
     for slot, (o, t) in enumerate(z_list):
@@ -242,8 +242,7 @@
     target_adj = tc_ref[...] - total_of(2, nr)
 
     coef[...] = sigma * target_adj
-    matvec(s, 3)
-    exchange(3, False)
+    push(s, 3, False)
     halves(s, s_hi, s_lo)
     wait_bytes(ry_pair, bulk_r.at[0])
     for slot, (o, t) in enumerate(z_list):
@@ -252,8 +251,7 @@
     source_adj = sc_ref[...] - total_of(3, nc)
 
     coef[...] = rho * source_adj
-    matvec(rt, 4)
-    exchange(4, True)
+    push(rt, 4, True)
     cut = nz // 2
     for slot in range(cut):
         along_z(ry_send, ry_recv, slot, *z_list[slot], bulk_s.at[1], bulk_r.at[1])
@@ -262,24 +260,20 @@
     target_adj = tc_ref[...] - total_of(4, nr)
 
     coef[...] = sigma * target_adj
-    matvec(s, 5)
-    exchange(5, False)
-    for slot, (o, t) in enumerate(r_list[:-1]):
-        along_r(sx, sx_recv, slot, o, t, bulk_s.at[3], bulk_r.at[3])
+    push(s, 5, False)
+    fill_column(0, sc_ref)
     arrived(5, nc)
     source_adj = sc_ref[...] - total_of(5, nc)
 
     coef[...] = rho * source_adj
-    matvec(rt, 6)
-    exchange(6, True)
+    push(rt, 6, True)
     for slot in range(cut, nz - 1):
         along_z(ry_send, ry_recv, slot, *z_list[slot], bulk_s.at[2], bulk_r.at[2])
     arrived(6, nr)
     target_adj = tc_ref[...] - total_of(6, nr)
 
     coef[...] = sigma * target_adj
-    matvec(s, 7)
-    exchange(7, False)
+    push(s, 7, False)
     scale_points(yt)
     tall_c = cb * sub_c
 
@@ -300,6 +294,8 @@
         if n:
             z_forward(n - 1)
     z_forward(ch_c - 1)
+    fill_column(2, target_adj)
+    sx[...] = sx[...] * cols[2]
 
     arrived(7, nc)
     source_adj = sc_ref[...] - total_of(7, nc)
@@ -314,27 +310,18 @@
         acc = rt[rows, 0:128] * coef[0:1, :]
         for q in range(1, groups):
             acc = acc + rt[rows, q * 128:(q + 1) * 128] * coef[q:q + 1, :]
-        tp[rows, :] = y_ref[rows, :] * jnp.sum(acc, axis=1, keepdims=True) - moved
+        tp[rows, :] = y_ref[rows, :] * jnp.sum(acc, axis=1, keepdims=True) - moved - sx[rows, :]
         for slot in range(n * cb, (n + 1) * cb):
             if slot < nr - 1:
                 along_r(tp, tp_recv, slot, *r_list[slot], late_s.at[ch_c + 1], late_r.at[ch_c + 1])
 
-    for k in range(groups):
-        rows = slice(k * 128, (k + 1) * 128)
-        cols[0, rows, :] = column(sc_ref[k:k + 1, :])
-        cols[1, rows, :] = column(source_adj[k:k + 1, :])
-        cols[2, rows, :] = column(target_adj[k:k + 1, :])
-
+    fill_column(1, source_adj)
     own_c, own_r = block(c, sub_c), block(r, sub_r)
     wait_bytes(ry_recv.at[pl.ds(0, cut)], bulk_r.at[1])
     wait_bytes(ry_recv.at[pl.ds(cut, nz - 1 - cut)], bulk_r.at[2])
     moved = ry_send[nz - 1]
     for slot in range(nz - 1):
         moved = moved + ry_recv[slot]
-    wait_bytes(sx_recv, bulk_r.at[3])
-    other = sx[own_r, :]
-    for slot in range(nr - 1):
-        other = other + sx_recv[slot]
     wait_bytes(zp_recv, late_r.at[ch_c])
     late = zp_send[nz - 1]
     for slot in range(nz - 1):
@@ -344,21 +331,20 @@
     late = tp[own_r, :]
     for slot in range(nr - 1):
         late = late + tp_recv[slot]
-    gt_ref[...] = cols[2, own_r, :] * (y_ref[own_r, :] - other) + late
+    gt_ref[...] = cols[2, own_r, :] * y_ref[own_r, :] + late
 
     for slot, n in enumerate((nc, nr, nr, nc, nr, nc, nr, nc)):
         wait_bytes(recv.at[slot, pl.ds(0, n - 1)], ssem.at[slot])
     wait_bytes(ry_pair, bulk_s.at[0])
     wait_bytes(ry_recv.at[pl.ds(0, cut)], bulk_s.at[1])
     wait_bytes(ry_recv.at[pl.ds(cut, nz - 1 - cut)], bulk_s.at[2])
-    wait_bytes(sx_recv, bulk_s.at[3])
     for n in range(ch_c):
         wait_bytes(zp_pair.at[pl.ds(n * half, half)], late_s.at[n])
     wait_bytes(zp_recv, late_s.at[ch_c])
     wait_bytes(tp_recv, late_s.at[ch_c + 1])
 
 
-def shards(nr, nc, cb, lane_chunk, x, y, f, g, sc, tc):
+def shards(nr, nc, cb, lane_chunk, pieces, x, y, f, g, sc, tc):
     size = x.shape[0]
     groups = size // 128
     sub_r, sub_c = size // nr, size // nc
@@ -368,7 +354,7 @@
     nz = nc // 2
     square = (size, size)
     return pl.pallas_call(
-        functools.partial(kernel, nr, nc, cb, lane_chunk),
+        functools.partial(kernel, nr, nc, cb, lane_chunk, pieces),
         out_shape=(
             jax.ShapeDtypeStruct((sub_c, D), F32),
             jax.ShapeDtypeStruct((sub_r, D), F32),
@@ -400,7 +386,6 @@
             pltpu.VMEM((nz, sub_c, D), F32),
             pltpu.VMEM((nz - 1, sub_c, D), F32),
             pltpu.VMEM((size, D), F32),
-            pltpu.VMEM((nr - 1, sub_r, D), F32),
             pltpu.VMEM((size, D), F32),
             pltpu.VMEM((nz, sub_c, D), F32),
             pltpu.VMEM((nz, sub_c, D), F32),
@@ -408,8 +393,8 @@
             pltpu.VMEM((size, D), F32),
             pltpu.VMEM((nr - 1, sub_r, D), F32),
             pltpu.VMEM((3, size, D), F32),
-            pltpu.SemaphoreType.DMA((4,)),
-            pltpu.SemaphoreType.DMA((4,)),
+            pltpu.SemaphoreType.DMA((3,)),
+            pltpu.SemaphoreType.DMA((3,)),
             pltpu.SemaphoreType.DMA((nc // cb + 2,)),
             pltpu.SemaphoreType.DMA((nc // cb + 2,)),
         ],
@@ -419,8 +404,8 @@
     )(x, y, *vectors)
 
 
-def solution(mesh, cb=4, lane_chunk=256):
+def solution(mesh, cb=4, lane_chunk=256, pieces=1):
     in_specs = (P("row", None), P("col", None), P("row"), P("col"), P("row"), P("col"))
     out_specs = (P(("row", "col"), None), P(("col", "row"), None))
-    body = functools.partial(shards, mesh.shape["row"], mesh.shape["col"], cb, lane_chunk)
+    body = functools.partial(shards, mesh.shape["row"], mesh.shape["col"], cb, lane_chunk, pieces)
     return jax.shard_map(body, mesh=mesh, in_specs=in_specs, out_specs=out_specs, check_vma=False)

time: 82.8 us -> 70.9 us (0.86)
  Pallas kernels: 79.9 us -> 68 us
    pallas_call x1, Pallas kernels: 79.9 us -> 68 us  [shards(): pl.pallas_call(functools.partial(kernel, nr, nc, cb, lane_chunk, pieces),...]
where the time goes in v2:
time: 70.9 us; the launch traced here: 70.7 us
  Pallas kernels  68 us (96%)
  local copies, waits for them, and re-layouts  2.06 us (3%)
    pallas_call x1, Pallas kernels, shards(): pl.pallas_call(functools.partial(kernel, nr, nc, cb, lane_chunk, pieces),...  68 us
    unnamed x4, local copies, waits for them, and re-layouts  2.06 us

profile of v2, /device:TPU:1, one launch (start us, length us, event | category | flops | bytes accessed | tf_op | source)
XLA Modules:
  0.0 70.7 jit_solution(9187375843895511170)
XLA Ops:
  0.6 68.0 %shard_map.77 = (f32[96,128]{1,0:T(8,128)}, f32[96,128]{1,0:T(8,128)}) custom-call(f32[1536,128]{1,0:T(8,128)} %x_ref.1, f32[1536,128]{1,0:T(8,128)} %y_ref.1, f32[12,128]{1,0:T(8,128)} %bitcast.4, f32[12,128]{1,0:T(8,128)} %bitcast.5, f32[12,128]{1,0:T(8,128)} %bitcast.6, f32[12,128]{1,0:T(8,128)} %bitcast.7), custom_call_target="tpu_custom_call" | custom-call | tf_op jit(solution)/shard_map/pallas_call | solution.py:356
  68.6 0.0 copy-start
  68.6 1.4 %copy.10 = f32[96,128]{1,0:T(8,128)} copy(f32[96,128]{1,0:T(8,128)} %get-tuple-element.4) | data formatting | bytes 98304
  70.1 0.0 copy-done
  70.1 0.6 copy.11
Async XLA Ops:
  68.6 1.4 %copy-start = (f32[96,128]{1,0:T(8,128)S(1)}, f32[96,128]{1,0:T(8,128)}, u32[]{:S(2)}) copy-start(f32[96,128]{1,0:T(8,128)} %get-tuple-element.5) | copy-start | bytes 147460

commit v3 on v2

--- a/solution.py
+++ b/solution.py
@@ -31,7 +31,7 @@
 
 def kernel(
     nr, nc, cb, lane_chunk, pieces,
-    x_ref, y_ref, f_ref, g_ref, sc_ref, tc_ref, gs_ref, gt_ref,
+    x_ref, y_ref, f_ref, g_ref, sc_ref, tc_ref, out_ref,
     xc, yc, rt, s, rt_hi, rt_lo, s_hi, s_lo, xt, yt, xt2, yt2, scaled,
     peak, coef, send, recv, ssem, rsem,
     ry, ry_pair, ry_send, ry_recv, sx,
@@ -110,11 +110,17 @@
                             pl.semaphore_wait(barrier, nr + nc - 2)
                         exchange(round_slot, along_row, group + 1 - per)
 
+    def ring(n):
+        return lambda d: min(d % n, -d % n)
+
     def exchange(slot, along_row, first):
         n = nr if along_row else nc
-        order = sorted(range(1, n), key=lambda d: -min(d, n - d))
-        for d in order:
-            device = (lax.rem(r + d, n), c) if along_row else (r, lax.rem(c + d, n))
+        hops = (lambda d: ring(nr // cb)(d // cb) + ring(cb)(d % cb)) if along_row else ring(n)
+        for d in sorted(range(1, n), key=lambda d: -hops(d)):
+            if along_row:
+                device = (lax.rem(r // cb + d // cb, nr // cb) * cb + lax.rem(r + d % cb, cb), c)
+            else:
+                device = (r, lax.rem(c + d, nc))
             pltpu.make_async_remote_copy(
                 send.at[slot, pl.ds(first, per)], recv.at[slot, d - 1, pl.ds(first, per)],
                 ssem.at[slot], rsem.at[slot], device_id=device, device_id_type=MESH,
@@ -185,34 +191,31 @@
             lanes = slice(k * 128, (k + 1) * 128)
             scaled[0:D, lanes], scaled[D:2 * D, lanes] = split(points[:, lanes] * coef[k:k + 1, :])
 
-    half = cb // 2
-    ch_c, ch_r = nc // cb, nr // cb
-
-    def offsets(n):
-        return sorted(range(n), key=lambda o: -min(o, n - o))
-
-    def z_dest(o, t):
-        return lax.rem(z // half + o, ch_c) * half + lax.rem(z + t, half)
+    nz = nc // 2
+    z_late = [nz // 2, 1] + [e for d in range(nz // 2 - 1, 1, -1) for e in (d, nz - d)] + [nz - 1, 0]
+    z_early = sorted(range(nz), key=lambda d: (2 if d == 0 else 1 - d % 2, -min(d, nz - d)))
+    ch_r = nr // cb
+    r_list = [(o, t) for o in sorted(range(ch_r), key=lambda o: -min(o, ch_r - o)) for t in reversed(range(cb))]
+
+    def z_dest(d):
+        return lax.rem(z + d, nz)
 
     def r_dest(o, t):
         return lax.rem(r // cb + o, ch_r) * cb + lax.rem(r + t, cb)
 
-    z_list = [(o, t) for o in offsets(ch_c) for t in reversed(range(half))]
-    r_list = [(o, t) for o in offsets(ch_r) for t in reversed(range(cb))]
-
     def block(index, rows):
         return pl.ds(pl.multiple_of(index * rows, 8), rows)
 
-    def to_partner(source, pair, slot, o, t, s_sem, r_sem):
+    def to_partner(source, pair, slot, d, s_sem, r_sem):
         pltpu.make_async_remote_copy(
-            source.at[block(z_dest(o, t) * 2 + 1 - h, sub_c)], pair.at[slot], s_sem, r_sem,
+            source.at[block(z_dest(d) * 2 + 1 - h, sub_c)], pair.at[slot], s_sem, r_sem,
             device_id=(r, z * 2 + 1 - h), device_id_type=MESH,
         ).start()
 
-    def along_z(out, inbox, slot, o, t, s_sem, r_sem):
+    def along_z(out, inbox, slot, d, s_sem, r_sem):
         pltpu.make_async_remote_copy(
             out.at[slot], inbox.at[slot], s_sem, r_sem,
-            device_id=(r, z_dest(o, t) * 2 + h), device_id_type=MESH,
+            device_id=(r, z_dest(d) * 2 + h), device_id_type=MESH,
         ).start()
 
     def along_r(source, inbox, slot, o, t, s_sem, r_sem):
@@ -220,8 +223,6 @@
             source.at[block(r_dest(o, t), sub_r)], inbox.at[slot], s_sem, r_sem,
             device_id=(r_dest(o, t), c), device_id_type=MESH,
         ).start()
-
-    nz = nc // 2
 
     soften(yc, xc, rt, 0, 0, False)
     soften(xc, yc, s, 1, 1, True)
@@ -234,8 +235,8 @@
     push(rt, 2, True)
     halves(rt, rt_hi, rt_lo)
     early(yt2, rt_hi, rt_lo, rho, ry)
-    for slot, (o, t) in enumerate(z_list):
-        to_partner(ry, ry_pair, slot, o, t, bulk_s.at[0], bulk_r.at[0])
+    for slot, d in enumerate(z_early):
+        to_partner(ry, ry_pair, slot, d, bulk_s.at[0], bulk_r.at[0])
     arrived(1, nr)
     sigma = norm_scale(1, nr, 1)
     arrived(2, nr)
@@ -245,8 +246,8 @@
     push(s, 3, False)
     halves(s, s_hi, s_lo)
     wait_bytes(ry_pair, bulk_r.at[0])
-    for slot, (o, t) in enumerate(z_list):
-        ry_send[slot] = ry[block(z_dest(o, t) * 2 + h, sub_c), :] + ry_pair[slot]
+    for slot, d in enumerate(z_early):
+        ry_send[slot] = ry[block(z_dest(d) * 2 + h, sub_c), :] + ry_pair[slot]
     arrived(3, nc)
     source_adj = sc_ref[...] - total_of(3, nc)
 
@@ -254,7 +255,7 @@
     push(rt, 4, True)
     cut = nz // 2
     for slot in range(cut):
-        along_z(ry_send, ry_recv, slot, *z_list[slot], bulk_s.at[1], bulk_r.at[1])
+        along_z(ry_send, ry_recv, slot, z_early[slot], bulk_s.at[1], bulk_r.at[1])
     early(xt2, s_hi, s_lo, sigma, sx)
     arrived(4, nr)
     target_adj = tc_ref[...] - total_of(4, nr)
@@ -268,32 +269,33 @@
     coef[...] = rho * source_adj
     push(rt, 6, True)
     for slot in range(cut, nz - 1):
-        along_z(ry_send, ry_recv, slot, *z_list[slot], bulk_s.at[2], bulk_r.at[2])
+        along_z(ry_send, ry_recv, slot, z_early[slot], bulk_s.at[2], bulk_r.at[2])
     arrived(6, nr)
     target_adj = tc_ref[...] - total_of(6, nr)
 
     coef[...] = sigma * target_adj
     push(s, 7, False)
     scale_points(yt)
-    tall_c = cb * sub_c
 
     def z_forward(n):
-        wait_bytes(zp_pair.at[pl.ds(n * half, half)], late_r.at[n])
-        for slot in range(n * half, (n + 1) * half):
-            o, t = z_list[slot]
-            zp_send[slot] = zp[block(z_dest(o, t) * 2 + h, sub_c), :] + zp_pair[slot]
+        wait_bytes(zp_pair.at[pl.ds(2 * n, 2)], late_r.at[n])
+        for slot in (2 * n, 2 * n + 1):
+            zp_send[slot] = zp[block(z_dest(z_late[slot]) * 2 + h, sub_c), :] + zp_pair[slot]
             if slot < nz - 1:
-                along_z(zp_send, zp_recv, slot, o, t, late_s.at[ch_c], late_r.at[ch_c])
-
-    for n in range(ch_c):
-        rows = block(lax.rem(z // half + z_list[n * half][0], ch_c), tall_c)
-        both = mm(s_hi[rows, :], scaled[...], NT)
-        zp[rows, :] = both[:, 0:D] + both[:, D:2 * D] + mm(s_lo[rows, :], scaled[0:D, :], NT)
-        for slot in range(n * half, (n + 1) * half):
-            to_partner(zp, zp_pair, slot, *z_list[slot], late_s.at[n], late_r.at[n])
+                along_z(zp_send, zp_recv, slot, z_late[slot], late_s.at[nz // 2], late_r.at[nz // 2])
+
+    for n in range(nz // 2):
+        pair = [block(z_dest(z_late[slot]), 2 * sub_c) for slot in (2 * n, 2 * n + 1)]
+        both = mm(jnp.concatenate([s_hi[rows, :] for rows in pair]), scaled[...], NT)
+        moved = both[:, 0:D] + both[:, D:2 * D]
+        moved = moved + mm(jnp.concatenate([s_lo[rows, :] for rows in pair]), scaled[0:D, :], NT)
+        for place, rows in enumerate(pair):
+            zp[rows, :] = moved[2 * sub_c * place:2 * sub_c * (place + 1)]
+        for slot in (2 * n, 2 * n + 1):
+            to_partner(zp, zp_pair, slot, z_late[slot], late_s.at[n], late_r.at[n])
         if n:
             z_forward(n - 1)
-    z_forward(ch_c - 1)
+    z_forward(nz // 2 - 1)
     fill_column(2, target_adj)
     sx[...] = sx[...] * cols[2]
 
@@ -313,7 +315,7 @@
         tp[rows, :] = y_ref[rows, :] * jnp.sum(acc, axis=1, keepdims=True) - moved - sx[rows, :]
         for slot in range(n * cb, (n + 1) * cb):
             if slot < nr - 1:
-                along_r(tp, tp_recv, slot, *r_list[slot], late_s.at[ch_c + 1], late_r.at[ch_c + 1])
+                along_r(tp, tp_recv, slot, *r_list[slot], late_s.at[nz // 2 + 1], late_r.at[nz // 2 + 1])
 
     fill_column(1, source_adj)
     own_c, own_r = block(c, sub_c), block(r, sub_r)
@@ -322,26 +324,26 @@
     moved = ry_send[nz - 1]
     for slot in range(nz - 1):
         moved = moved + ry_recv[slot]
-    wait_bytes(zp_recv, late_r.at[ch_c])
+    wait_bytes(zp_recv, late_r.at[nz // 2])
     late = zp_send[nz - 1]
     for slot in range(nz - 1):
         late = late + zp_recv[slot]
-    gs_ref[...] = x_ref[own_c, :] * cols[0, own_c, :] - cols[1, own_c, :] * moved - late
-    wait_bytes(tp_recv, late_r.at[ch_c + 1])
+    out_ref[0:sub_c, :] = x_ref[own_c, :] * cols[0, own_c, :] - cols[1, own_c, :] * moved - late
+    wait_bytes(tp_recv, late_r.at[nz // 2 + 1])
     late = tp[own_r, :]
     for slot in range(nr - 1):
         late = late + tp_recv[slot]
-    gt_ref[...] = cols[2, own_r, :] * y_ref[own_r, :] + late
+    out_ref[sub_c:sub_c + sub_r, :] = cols[2, own_r, :] * y_ref[own_r, :] + late
 
     for slot, n in enumerate((nc, nr, nr, nc, nr, nc, nr, nc)):
         wait_bytes(recv.at[slot, pl.ds(0, n - 1)], ssem.at[slot])
     wait_bytes(ry_pair, bulk_s.at[0])
     wait_bytes(ry_recv.at[pl.ds(0, cut)], bulk_s.at[1])
     wait_bytes(ry_recv.at[pl.ds(cut, nz - 1 - cut)], bulk_s.at[2])
-    for n in range(ch_c):
-        wait_bytes(zp_pair.at[pl.ds(n * half, half)], late_s.at[n])
-    wait_bytes(zp_recv, late_s.at[ch_c])
-    wait_bytes(tp_recv, late_s.at[ch_c + 1])
+    for n in range(nz // 2):
+        wait_bytes(zp_pair.at[pl.ds(2 * n, 2)], late_s.at[n])
+    wait_bytes(zp_recv, late_s.at[nz // 2])
+    wait_bytes(tp_recv, late_s.at[nz // 2 + 1])
 
 
 def shards(nr, nc, cb, lane_chunk, pieces, x, y, f, g, sc, tc):
@@ -353,14 +355,11 @@
     peers = max(nr, nc) - 1
     nz = nc // 2
     square = (size, size)
-    return pl.pallas_call(
+    both = pl.pallas_call(
         functools.partial(kernel, nr, nc, cb, lane_chunk, pieces),
-        out_shape=(
-            jax.ShapeDtypeStruct((sub_c, D), F32),
-            jax.ShapeDtypeStruct((sub_r, D), F32),
-        ),
+        out_shape=jax.ShapeDtypeStruct((sub_c + sub_r, D), F32),
         in_specs=[vmem] * 6,
-        out_specs=(vmem, vmem),
+        out_specs=vmem,
         scratch_shapes=[
             pltpu.VMEM((size, 4 * D), BF16),
             pltpu.VMEM((size, 4 * D), BF16),
@@ -395,13 +394,14 @@
             pltpu.VMEM((3, size, D), F32),
             pltpu.SemaphoreType.DMA((3,)),
             pltpu.SemaphoreType.DMA((3,)),
-            pltpu.SemaphoreType.DMA((nc // cb + 2,)),
-            pltpu.SemaphoreType.DMA((nc // cb + 2,)),
+            pltpu.SemaphoreType.DMA((nz // 2 + 2,)),
+            pltpu.SemaphoreType.DMA((nz // 2 + 2,)),
         ],
         compiler_params=pltpu.CompilerParams(
             collective_id=0, has_side_effects=True, vmem_limit_bytes=62 << 20
         ),
     )(x, y, *vectors)
+    return both[:sub_c], both[sub_c:]
 
 
 def solution(mesh, cb=4, lane_chunk=256, pieces=1):

time: 70.9 us -> 66.8 us (0.942)
  Pallas kernels: 68 us -> 64.5 us
    pallas_call x1, Pallas kernels: 68 us -> 64.5 us  [shards(): pl.pallas_call(functools.partial(kernel, nr, nc, cb, lane_chunk, pieces),...]
    unnamed x4 -> x0, local copies, waits for them, and re-layouts: 2.06 us -> none
    slice x0 -> x1, local copies, waits for them, and re-layouts: none -> 1.46 us  [shards(): return (both[:sub_c], both[sub_c:])]
where the time goes in v3:
time: 66.8 us; the launch traced here: 66.6 us
  Pallas kernels  64.5 us (97%)
  local copies, waits for them, and re-layouts  1.46 us (2%)
    pallas_call x1, Pallas kernels, shards(): pl.pallas_call(functools.partial(kernel, nr, nc, cb, lane_chunk, pieces),...  64.5 us
    slice x1, local copies, waits for them, and re-layouts, shards(): return (both[:sub_c], both[sub_c:])  1.46 us

profile of v3, /device:TPU:1, one launch (start us, length us, event | category | flops | bytes accessed | tf_op | source)
XLA Modules:
  0.0 66.6 jit_solution(2286940833959740582)
XLA Ops:
  0.6 64.5 %shard_map.77 = f32[192,128]{1,0:T(8,128)} custom-call(f32[1536,128]{1,0:T(8,128)} %x_ref.1, f32[1536,128]{1,0:T(8,128)} %y_ref.1, f32[12,128]{1,0:T(8,128)} %bitcast.4, f32[12,128]{1,0:T(8,128)} %bitcast.5, f32[12,128]{1,0:T(8,128)} %bitcast.6, f32[12,128]{1,0:T(8,128)} %bitcast.7), custom_call_target="tpu_custom_call" | custom-call | tf_op jit(solution)/shard_map/pallas_call | solution.py:358
  65.2 1.5 %fusion = (f32[96,128]{1,0:T(8,128)}, f32[96,128]{1,0:T(8,128)}) fusion(f32[192,128]{1,0:T(8,128)} %shard_map.77), kind=kLoop, calls=%fused_computation | loop fusion | bytes 196608 | tf_op jit(solution)/shard_map/slice | solution.py:404

commit v4 on v3

--- a/solution.py
+++ b/solution.py
@@ -293,11 +293,11 @@
             zp[rows, :] = moved[2 * sub_c * place:2 * sub_c * (place + 1)]
         for slot in (2 * n, 2 * n + 1):
             to_partner(zp, zp_pair, slot, z_late[slot], late_s.at[n], late_r.at[n])
-        if n:
-            z_forward(n - 1)
-    z_forward(nz // 2 - 1)
+        if n > 1:
+            z_forward(n - 2)
     fill_column(2, target_adj)
     sx[...] = sx[...] * cols[2]
+    z_forward(nz // 2 - 2)
 
     arrived(7, nc)
     source_adj = sc_ref[...] - total_of(7, nc)
@@ -316,6 +316,8 @@
         for slot in range(n * cb, (n + 1) * cb):
             if slot < nr - 1:
                 along_r(tp, tp_recv, slot, *r_list[slot], late_s.at[nz // 2 + 1], late_r.at[nz // 2 + 1])
+        if n == 0:
+            z_forward(nz // 2 - 1)
 
     fill_column(1, source_adj)
     own_c, own_r = block(c, sub_c), block(r, sub_r)

time: 66.8 us -> 65.8 us (0.985)
  Pallas kernels: 64.5 us -> 63.6 us
    pallas_call x1, Pallas kernels: 64.5 us -> 63.6 us  [shards(): pl.pallas_call(functools.partial(kernel, nr, nc, cb, lane_chunk, pieces),...]
where the time goes in v4:
time: 65.8 us; the launch traced here: 65.7 us
  Pallas kernels  63.6 us (97%)
  local copies, waits for them, and re-layouts  1.46 us (2%)
    pallas_call x1, Pallas kernels, shards(): pl.pallas_call(functools.partial(kernel, nr, nc, cb, lane_chunk, pieces),...  63.6 us
    slice x1, local copies, waits for them, and re-layouts, shards(): return (both[:sub_c], both[sub_c:])  1.46 us

profile of v4, /device:TPU:1, one launch (start us, length us, event | category | flops | bytes accessed | tf_op | source)
XLA Modules:
  0.0 65.7 jit_solution(9524334038101935673)
XLA Ops:
  0.6 63.6 %shard_map.77 = f32[192,128]{1,0:T(8,128)} custom-call(f32[1536,128]{1,0:T(8,128)} %x_ref.1, f32[1536,128]{1,0:T(8,128)} %y_ref.1, f32[12,128]{1,0:T(8,128)} %bitcast.4, f32[12,128]{1,0:T(8,128)} %bitcast.5, f32[12,128]{1,0:T(8,128)} %bitcast.6, f32[12,128]{1,0:T(8,128)} %bitcast.7), custom_call_target="tpu_custom_call" | custom-call | tf_op jit(solution)/shard_map/pallas_call | solution.py:360
  64.2 1.5 %fusion = (f32[96,128]{1,0:T(8,128)}, f32[96,128]{1,0:T(8,128)}) fusion(f32[192,128]{1,0:T(8,128)} %shard_map.77), kind=kLoop, calls=%fused_computation | loop fusion | bytes 196608 | tf_op jit(solution)/shard_map/slice | solution.py:406

commit v5 on v4

--- a/solution.py
+++ b/solution.py
@@ -186,7 +186,7 @@
         for k in range(groups):
             cols[slot, k * 128:(k + 1) * 128, :] = column(rows_of[k:k + 1, :])
 
-    def scale_points(points):
+    def scale_points(points, scaled):
         for k in range(groups):
             lanes = slice(k * 128, (k + 1) * 128)
             scaled[0:D, lanes], scaled[D:2 * D, lanes] = split(points[:, lanes] * coef[k:k + 1, :])
@@ -275,7 +275,7 @@
 
     coef[...] = sigma * target_adj
     push(s, 7, False)
-    scale_points(yt)
+    scale_points(yt, scaled)
 
     def z_forward(n):
         wait_bytes(zp_pair.at[pl.ds(2 * n, 2)], late_r.at[n])
@@ -284,7 +284,7 @@
             if slot < nz - 1:
                 along_z(zp_send, zp_recv, slot, z_late[slot], late_s.at[nz // 2], late_r.at[nz // 2])
 
-    for n in range(nz // 2):
+    def z_block(n):
         pair = [block(z_dest(z_late[slot]), 2 * sub_c) for slot in (2 * n, 2 * n + 1)]
         both = mm(jnp.concatenate([s_hi[rows, :] for rows in pair]), scaled[...], NT)
         moved = both[:, 0:D] + both[:, D:2 * D]
@@ -293,22 +293,26 @@
             zp[rows, :] = moved[2 * sub_c * place:2 * sub_c * (place + 1)]
         for slot in (2 * n, 2 * n + 1):
             to_partner(zp, zp_pair, slot, z_late[slot], late_s.at[n], late_r.at[n])
+
+    for n in range(nz // 2 - 1):
+        z_block(n)
         if n > 1:
             z_forward(n - 2)
     fill_column(2, target_adj)
     sx[...] = sx[...] * cols[2]
-    z_forward(nz // 2 - 2)
+    if nz // 2 > 2:
+        z_forward(nz // 2 - 3)
 
     arrived(7, nc)
     source_adj = sc_ref[...] - total_of(7, nc)
 
     coef[...] = rho * source_adj
-    scale_points(xt)
+    scale_points(xt, xt2)
     tall_r = cb * sub_r
     for n in range(ch_r):
         rows = block(lax.rem(r // cb + r_list[n * cb][0], ch_r), tall_r)
-        both = mm(rt_hi[rows, :], scaled[...], NT)
-        moved = both[:, 0:D] + both[:, D:2 * D] + mm(rt_lo[rows, :], scaled[0:D, :], NT)
+        both = mm(rt_hi[rows, :], xt2[...], NT)
+        moved = both[:, 0:D] + both[:, D:2 * D] + mm(rt_lo[rows, :], xt2[0:D, :], NT)
         acc = rt[rows, 0:128] * coef[0:1, :]
         for q in range(1, groups):
             acc = acc + rt[rows, q * 128:(q + 1) * 128] * coef[q:q + 1, :]
@@ -317,6 +321,9 @@
             if slot < nr - 1:
                 along_r(tp, tp_recv, slot, *r_list[slot], late_s.at[nz // 2 + 1], late_r.at[nz // 2 + 1])
         if n == 0:
+            z_block(nz // 2 - 1)
+            z_forward(nz // 2 - 2)
+        if n == ch_r - 1:
             z_forward(nz // 2 - 1)
 
     fill_column(1, source_adj)

time: 65.8 us -> 65.9 us (level)
  no operation moved by 1% of the time
where the time goes in v5:
time: 65.9 us; the launch traced here: 65.7 us
  Pallas kernels  63.6 us (97%)
  local copies, waits for them, and re-layouts  1.46 us (2%)
    pallas_call x1, Pallas kernels, shards(): pl.pallas_call(functools.partial(kernel, nr, nc, cb, lane_chunk, pieces),...  63.6 us
    slice x1, local copies, waits for them, and re-layouts, shards(): return (both[:sub_c], both[sub_c:])  1.46 us

profile of v5, /device:TPU:1, one launch (start us, length us, event | category | flops | bytes accessed | tf_op | source)
XLA Modules:
  0.0 65.7 jit_solution(11601111126728184230)
XLA Ops:
  0.6 63.6 %shard_map.77 = f32[192,128]{1,0:T(8,128)} custom-call(f32[1536,128]{1,0:T(8,128)} %x_ref.1, f32[1536,128]{1,0:T(8,128)} %y_ref.1, f32[12,128]{1,0:T(8,128)} %bitcast.4, f32[12,128]{1,0:T(8,128)} %bitcast.5, f32[12,128]{1,0:T(8,128)} %bitcast.6, f32[12,128]{1,0:T(8,128)} %bitcast.7), custom_call_target="tpu_custom_call" | custom-call | tf_op jit(solution)/shard_map/pallas_call | solution.py:367
  64.2 1.5 %fusion = (f32[96,128]{1,0:T(8,128)}, f32[96,128]{1,0:T(8,128)}) fusion(f32[192,128]{1,0:T(8,128)} %shard_map.77), kind=kLoop, calls=%fused_computation | loop fusion | bytes 196608 | tf_op jit(solution)/shard_map/slice | solution.py:413
